TPU v7x, 32 devices: a whole 2x2x4 slice. The times are simulated.
32 devices in a mesh: parts: 2 (over y), span: 4 (over x, core), seq: 4 (over z).
Axes of the slice: x: 2, y: 2, z: 4, core: 2. Of those that a mesh axis runs over, the one named last changes fastest.
Arguments:
- q_in: bfloat16 [8, 1024, 4096], P(('parts', 'span'), 'seq'), parts along dimension 0, may hold values from -9 to 9
- k_in: bfloat16 [8, 1024, 4096], P(('parts', 'span'), 'seq'), parts along dimension 0, may hold values from -9 to 9
- v_in: bfloat16 [8, 1024, 4096], P(('parts', 'span'), 'seq'), parts along dimension 0, may hold values from -18 to 18
- timesteps: int32 [8], P('parts'), parts along dimension 0, may hold values from 0 to 31
- gate_table: float32 [32, 4096], replicated, may hold values from 0.1 to 1.9
Outputs:
- gated_out: bfloat16 [8, 1024, 4096], P(('parts', 'span'), 'seq'), parts along dimension 0
There are 2 independent parts, one for each index of `parts`. A program takes and returns all parts, laid end to end along the dimension named above; an argument that names none is the same for every part. Nothing has to cross between parts.
All inputs are finite; a program needn't handle non-finite values.
Results may differ from a plain program's by a relative error of at most 0.0053.
Values may be sent and summed in bfloat16 or wider, within the bound.
A program may use at most 128 MiB of HBM per device.

v0:
```python
import math
import jax
import jax.numpy as jnp
from jax import lax
from jax.sharding import PartitionSpec as P

HD = 128
masked_score = -1e30


def local(q_in, k_in, v_in, timesteps, gate_table):
    head_rows, key_rows, value_rows = (
        lax.all_to_all(q_in[0], "seq", split_axis=1, concat_axis=0, tiled=True),
        lax.all_to_all(k_in[0], "seq", split_axis=1, concat_axis=0, tiled=True),
        lax.all_to_all(v_in[0], "seq", split_axis=1, concat_axis=0, tiled=True),
    )
    length = head_rows.shape[0]
    columns = head_rows.shape[1]
    heads = columns // HD
    scale = HD ** (-0.5)
    span_id = lax.axis_index("span")
    limit = (span_id + 1) * length
    query_three = head_rows.reshape(length, heads, HD)
    init = (
        jnp.full((heads, length), masked_score, jnp.float32),
        jnp.zeros((heads, length), jnp.float32),
        jnp.zeros((length, heads, HD), jnp.float32),
    )
    key_piece = lax.all_gather(key_rows, "span", axis=0, tiled=True)
    value_piece = lax.all_gather(value_rows, "span", axis=0, tiled=True)
    count = key_piece.shape[0]
    block = math.gcd(count, 512)

    def one_block(index, state):
        top, total, accum = state
        offset = index * block
        key_block = lax.dynamic_slice_in_dim(key_piece, offset, block, 0).reshape(block, heads, HD)
        value_block = lax.dynamic_slice_in_dim(value_piece, offset, block, 0).reshape(
            block, heads, HD
        )
        scores = (
            jnp.einsum("qhd,khd->hqk", query_three, key_block, preferred_element_type=jnp.float32)
            * scale
        )
        keep = offset + jnp.arange(block) < limit
        scores = jnp.where(keep[None, None, :], scores, masked_score)
        new_top = jnp.maximum(top, jnp.max(scores, axis=-1))
        expo = jnp.where(keep[None, None, :], jnp.exp(scores - new_top[:, :, None]), 0.0)
        shrink = jnp.exp(top - new_top)
        total = total * shrink + jnp.sum(expo, axis=-1)
        mixed = jnp.einsum(
            "hqk,khd->qhd",
            expo.astype(jnp.bfloat16),
            value_block,
            preferred_element_type=jnp.float32,
        )
        accum = accum * shrink.T[:, :, None] + mixed
        return (new_top, total, accum)

    def run_blocks(state):
        return lax.fori_loop(0, count // block, one_block, state)

    def keep_state(state):
        return state

    top, total, accum = lax.cond(jnp.int32(0) < limit, run_blocks, keep_state, init)
    attn = (accum / total.T[:, :, None]).reshape(length, columns).astype(jnp.bfloat16)
    token_rows = lax.all_to_all(attn, "seq", split_axis=0, concat_axis=1, tiled=True)
    steps_count = gate_table.shape[0]
    span_step = lax.dynamic_index_in_dim(timesteps, span_id, 0, keepdims=False)
    picked = (jnp.arange(steps_count) == span_step).astype(jnp.float32)
    gate = jnp.dot(picked, gate_table, precision=lax.Precision.HIGHEST)
    return (token_rows.astype(jnp.float32) * gate[None, :]).astype(jnp.bfloat16)[None]


def solution(mesh):
    in_specs = (
        P(("parts", "span"), "seq", None),
        P(("parts", "span"), "seq", None),
        P(("parts", "span"), "seq", None),
        P("parts"),
        P(),
    )
    out_specs = P(("parts", "span"), "seq", None)
    return jax.shard_map(local, mesh=mesh, in_specs=in_specs, out_specs=out_specs, check_vma=False)
```

profile of v0, /device:TPU:0, one launch (start us, length us, event | category | flops | bytes accessed | tf_op | source)
XLA Modules:
  0.0 533.7 jit_solution(13859830746761117424)
XLA Ops:
  10.7 54.5 %all_to_all.64 = bf16[256,4,1024]{0,2,1:T(8,128)(2,1)S(1)} all-to-all(bf16[256,4,1024]{0,2,1:T(8,128)(2,1)} %bitcast.80), channel_id=1, replica_groups=mesh['parts'=2,'span'=4,'seq'=4] {'seq'}, dimensions={1} | all-to-all | bytes 4194304 | tf_op jit(solution)/shard_map/all_to_all | solution.py:14
  71.8 51.0 %all_to_all.65 = bf16[256,4,1024]{0,2,1:T(8,128)(2,1)S(1)} all-to-all(bf16[256,4,1024]{0,2,1:T(8,128)(2,1)} %bitcast.81), channel_id=1, replica_groups=mesh['parts'=2,'span'=4,'seq'=4] {'seq'}, dimensions={1} | all-to-all | bytes 4194304 | tf_op jit(solution)/shard_map/all_to_all | solution.py:15
  132.9 47.3 %all-to-all-done = bf16[256,4,1024]{0,2,1:T(8,128)(2,1)S(1)} async-done(((bf16[256,4,1024]{0,2,1:T(8,128)(2,1)}), bf16[256,4,1024]{0,2,1:T(8,128)(2,1)S(1)}, u32[]{:S(2)}, u32[]{:S(2)}) %all-to-all-start) | async-done | bytes 2097184 | tf_op jit(solution)/shard_map/all_to_all | solution.py:13
  180.2 5.0 all-gather.5.cloned.1.call-done
  185.2 271.6 %conditional.1 = (f32[8,1024]{1,0:T(8,128)}, f32[1024,8,128]{0,2,1:T(8,128)}) conditional(s32[]{:T(128)} %convert_element_type.44, () %tuple.27, (bf16[4,256,1024]{1,2,0:T(8,128)(2,1)S(1)}, s32[]{:T(128)}, bf16[4096,1024]{1,0:T(8,128)(2,1)}, bf16[4096,1024]{1,0:T(8,128)(2,1)}) %tuple.65), branch_computations={%region_0.0_spmd, %region_1.6_spmd} | conditional | flops 2205205504 | bytes 151521616 | solution.py:66
  191.5 265.3 %while.17 = (s32[]{:T(128)}, f32[8,1024]{1,0:T(8,128)S(1)}, f32[8,1024]{1,0:T(8,128)}, f32[1024,8,128]{0,2,1:T(8,128)}, s32[]{:T(128)}, /*index=5*/bf16[4096,102...) while((s32[]{:T(128)}, f32[8,1024]{1,0:T(8,128)S(1)}, ...), condition=%wide.region_5.5_spmd.clone, body=%wide.region_2.4_spmd.clone.sunk | while | flops 2205205504 | bytes 138938576 | solution.py:61
  195.7 9.4 %bitcast_reduce_fusion.2 = (f32[8,1024]{1,0:T(8,128)S(1)}, f32[8,512,1024]{2,1,0:T(8,128)}) fusion(pred[512]{0:T(512)(128)(4,1)S(1)} %add_compare_fusion.2, bf16[512,8,128]{0,2,1:T(8,128)(2,1)S(1)} %bitcast.72, bf16[1024,8,128]{2,0,1:T(8,128)(2,1)} %get-tuple-element.338), kind=kOutput, calls=%fused_computation.1.clone.1 | convolution fusion | flops 1086316544 | bytes 19956224 | tf_op jit(solution)/shard_map/cond/branch_1_fun/while/body/eval_jaxpr/qhd,khd->hqk/dot_general | solution.py:42
  205.6 10.9 %bitcast_add_fusion.2 = f32[1024,8,128]{0,2,1:T(8,128)} fusion(f32[1024,8,128]{0,2,1:T(8,128)} %get-tuple-element.323, bf16[512,8,128]{0,2,1:T(8,128)(2,1)S(1)} %bitcast.73, f32[8,512,1024]{2,1,0:T(8,128)} %get-tuple-element.305, f32[8,1024]{1,0:T(8,128)S(1)} %get-tuple-element.333, pred[512]{0:T(512)(128)(4,1)S(1)} %add_compare_fusion.2, ...), kind=kOutput, calls=%fused_computation.10.clone.1 | convolution fusion | flops 1097859072 | bytes 26280448 | tf_op jit(solution)/shard_map/cond/branch_1_fun/while/body/eval_jaxpr/hqk,khd->qhd/dot_general | solution.py:51
  227.1 9.4 %bitcast_reduce_fusion.2 = (f32[8,1024]{1,0:T(8,128)S(1)}, f32[8,512,1024]{2,1,0:T(8,128)}) fusion(pred[512]{0:T(512)(128)(4,1)S(1)} %add_compare_fusion.2, bf16[512,8,128]{0,2,1:T(8,128)(2,1)S(1)} %bitcast.72, bf16[1024,8,128]{2,0,1:T(8,128)(2,1)} %get-tuple-element.338), kind=kOutput, calls=%fused_computation.1.clone.1 | convolution fusion | flops 1086316544 | bytes 19956224 | tf_op jit(solution)/shard_map/cond/branch_1_fun/while/body/eval_jaxpr/qhd,khd->hqk/dot_general | solution.py:42
  237.1 12.1 %bitcast_add_fusion.2 = f32[1024,8,128]{0,2,1:T(8,128)} fusion(f32[1024,8,128]{0,2,1:T(8,128)} %get-tuple-element.323, bf16[512,8,128]{0,2,1:T(8,128)(2,1)S(1)} %bitcast.73, f32[8,512,1024]{2,1,0:T(8,128)} %get-tuple-element.305, f32[8,1024]{1,0:T(8,128)S(1)} %get-tuple-element.333, pred[512]{0:T(512)(128)(4,1)S(1)} %add_compare_fusion.2, ...), kind=kOutput, calls=%fused_computation.10.clone.1 | convolution fusion | flops 1097859072 | bytes 26280448 | tf_op jit(solution)/shard_map/cond/branch_1_fun/while/body/eval_jaxpr/hqk,khd->qhd/dot_general | solution.py:51
  250.3 4.6 fusion.37
  260.5 9.4 %bitcast_reduce_fusion.2 = (f32[8,1024]{1,0:T(8,128)S(1)}, f32[8,512,1024]{2,1,0:T(8,128)}) fusion(pred[512]{0:T(512)(128)(4,1)S(1)} %add_compare_fusion.2, bf16[512,8,128]{0,2,1:T(8,128)(2,1)S(1)} %bitcast.72, bf16[1024,8,128]{2,0,1:T(8,128)(2,1)} %get-tuple-element.338), kind=kOutput, calls=%fused_computation.1.clone.1 | convolution fusion | flops 1086316544 | bytes 19956224 | tf_op jit(solution)/shard_map/cond/branch_1_fun/while/body/eval_jaxpr/qhd,khd->hqk/dot_general | solution.py:42
  270.5 12.1 %bitcast_add_fusion.2 = f32[1024,8,128]{0,2,1:T(8,128)} fusion(f32[1024,8,128]{0,2,1:T(8,128)} %get-tuple-element.323, bf16[512,8,128]{0,2,1:T(8,128)(2,1)S(1)} %bitcast.73, f32[8,512,1024]{2,1,0:T(8,128)} %get-tuple-element.305, f32[8,1024]{1,0:T(8,128)S(1)} %get-tuple-element.333, pred[512]{0:T(512)(128)(4,1)S(1)} %add_compare_fusion.2, ...), kind=kOutput, calls=%fused_computation.10.clone.1 | convolution fusion | flops 1097859072 | bytes 26280448 | tf_op jit(solution)/shard_map/cond/branch_1_fun/while/body/eval_jaxpr/hqk,khd->qhd/dot_general | solution.py:51
  293.9 9.4 %bitcast_reduce_fusion.2 = (f32[8,1024]{1,0:T(8,128)S(1)}, f32[8,512,1024]{2,1,0:T(8,128)}) fusion(pred[512]{0:T(512)(128)(4,1)S(1)} %add_compare_fusion.2, bf16[512,8,128]{0,2,1:T(8,128)(2,1)S(1)} %bitcast.72, bf16[1024,8,128]{2,0,1:T(8,128)(2,1)} %get-tuple-element.338), kind=kOutput, calls=%fused_computation.1.clone.1 | convolution fusion | flops 1086316544 | bytes 19956224 | tf_op jit(solution)/shard_map/cond/branch_1_fun/while/body/eval_jaxpr/qhd,khd->hqk/dot_general | solution.py:42
  303.9 12.1 %bitcast_add_fusion.2 = f32[1024,8,128]{0,2,1:T(8,128)} fusion(f32[1024,8,128]{0,2,1:T(8,128)} %get-tuple-element.323, bf16[512,8,128]{0,2,1:T(8,128)(2,1)S(1)} %bitcast.73, f32[8,512,1024]{2,1,0:T(8,128)} %get-tuple-element.305, f32[8,1024]{1,0:T(8,128)S(1)} %get-tuple-element.333, pred[512]{0:T(512)(128)(4,1)S(1)} %add_compare_fusion.2, ...), kind=kOutput, calls=%fused_computation.10.clone.1 | convolution fusion | flops 1097859072 | bytes 26280448 | tf_op jit(solution)/shard_map/cond/branch_1_fun/while/body/eval_jaxpr/hqk,khd->qhd/dot_general | solution.py:51
  327.4 9.4 %bitcast_reduce_fusion.2 = (f32[8,1024]{1,0:T(8,128)S(1)}, f32[8,512,1024]{2,1,0:T(8,128)}) fusion(pred[512]{0:T(512)(128)(4,1)S(1)} %add_compare_fusion.2, bf16[512,8,128]{0,2,1:T(8,128)(2,1)S(1)} %bitcast.72, bf16[1024,8,128]{2,0,1:T(8,128)(2,1)} %get-tuple-element.338), kind=kOutput, calls=%fused_computation.1.clone.1 | convolution fusion | flops 1086316544 | bytes 19956224 | tf_op jit(solution)/shard_map/cond/branch_1_fun/while/body/eval_jaxpr/qhd,khd->hqk/dot_general | solution.py:42
  337.3 12.1 %bitcast_add_fusion.2 = f32[1024,8,128]{0,2,1:T(8,128)} fusion(f32[1024,8,128]{0,2,1:T(8,128)} %get-tuple-element.323, bf16[512,8,128]{0,2,1:T(8,128)(2,1)S(1)} %bitcast.73, f32[8,512,1024]{2,1,0:T(8,128)} %get-tuple-element.305, f32[8,1024]{1,0:T(8,128)S(1)} %get-tuple-element.333, pred[512]{0:T(512)(128)(4,1)S(1)} %add_compare_fusion.2, ...), kind=kOutput, calls=%fused_computation.10.clone.1 | convolution fusion | flops 1097859072 | bytes 26280448 | tf_op jit(solution)/shard_map/cond/branch_1_fun/while/body/eval_jaxpr/hqk,khd->qhd/dot_general | solution.py:51
  360.8 9.4 %bitcast_reduce_fusion.2 = (f32[8,1024]{1,0:T(8,128)S(1)}, f32[8,512,1024]{2,1,0:T(8,128)}) fusion(pred[512]{0:T(512)(128)(4,1)S(1)} %add_compare_fusion.2, bf16[512,8,128]{0,2,1:T(8,128)(2,1)S(1)} %bitcast.72, bf16[1024,8,128]{2,0,1:T(8,128)(2,1)} %get-tuple-element.338), kind=kOutput, calls=%fused_computation.1.clone.1 | convolution fusion | flops 1086316544 | bytes 19956224 | tf_op jit(solution)/shard_map/cond/branch_1_fun/while/body/eval_jaxpr/qhd,khd->hqk/dot_general | solution.py:42
  370.7 12.1 %bitcast_add_fusion.2 = f32[1024,8,128]{0,2,1:T(8,128)} fusion(f32[1024,8,128]{0,2,1:T(8,128)} %get-tuple-element.323, bf16[512,8,128]{0,2,1:T(8,128)(2,1)S(1)} %bitcast.73, f32[8,512,1024]{2,1,0:T(8,128)} %get-tuple-element.305, f32[8,1024]{1,0:T(8,128)S(1)} %get-tuple-element.333, pred[512]{0:T(512)(128)(4,1)S(1)} %add_compare_fusion.2, ...), kind=kOutput, calls=%fused_computation.10.clone.1 | convolution fusion | flops 1097859072 | bytes 26280448 | tf_op jit(solution)/shard_map/cond/branch_1_fun/while/body/eval_jaxpr/hqk,khd->qhd/dot_general | solution.py:51
  394.2 9.4 %bitcast_reduce_fusion.2 = (f32[8,1024]{1,0:T(8,128)S(1)}, f32[8,512,1024]{2,1,0:T(8,128)}) fusion(pred[512]{0:T(512)(128)(4,1)S(1)} %add_compare_fusion.2, bf16[512,8,128]{0,2,1:T(8,128)(2,1)S(1)} %bitcast.72, bf16[1024,8,128]{2,0,1:T(8,128)(2,1)} %get-tuple-element.338), kind=kOutput, calls=%fused_computation.1.clone.1 | convolution fusion | flops 1086316544 | bytes 19956224 | tf_op jit(solution)/shard_map/cond/branch_1_fun/while/body/eval_jaxpr/qhd,khd->hqk/dot_general | solution.py:42
  404.1 12.1 %bitcast_add_fusion.2 = f32[1024,8,128]{0,2,1:T(8,128)} fusion(f32[1024,8,128]{0,2,1:T(8,128)} %get-tuple-element.323, bf16[512,8,128]{0,2,1:T(8,128)(2,1)S(1)} %bitcast.73, f32[8,512,1024]{2,1,0:T(8,128)} %get-tuple-element.305, f32[8,1024]{1,0:T(8,128)S(1)} %get-tuple-element.333, pred[512]{0:T(512)(128)(4,1)S(1)} %add_compare_fusion.2, ...), kind=kOutput, calls=%fused_computation.10.clone.1 | convolution fusion | flops 1097859072 | bytes 26280448 | tf_op jit(solution)/shard_map/cond/branch_1_fun/while/body/eval_jaxpr/hqk,khd->qhd/dot_general | solution.py:51
  427.6 9.4 %bitcast_reduce_fusion.2 = (f32[8,1024]{1,0:T(8,128)S(1)}, f32[8,512,1024]{2,1,0:T(8,128)}) fusion(pred[512]{0:T(512)(128)(4,1)S(1)} %add_compare_fusion.2, bf16[512,8,128]{0,2,1:T(8,128)(2,1)S(1)} %bitcast.72, bf16[1024,8,128]{2,0,1:T(8,128)(2,1)} %get-tuple-element.338), kind=kOutput, calls=%fused_computation.1.clone.1 | convolution fusion | flops 1086316544 | bytes 19956224 | tf_op jit(solution)/shard_map/cond/branch_1_fun/while/body/eval_jaxpr/qhd,khd->hqk/dot_general | solution.py:42
  437.5 12.1 %bitcast_add_fusion.2 = f32[1024,8,128]{0,2,1:T(8,128)} fusion(f32[1024,8,128]{0,2,1:T(8,128)} %get-tuple-element.323, bf16[512,8,128]{0,2,1:T(8,128)(2,1)S(1)} %bitcast.73, f32[8,512,1024]{2,1,0:T(8,128)} %get-tuple-element.305, f32[8,1024]{1,0:T(8,128)S(1)} %get-tuple-element.333, pred[512]{0:T(512)(128)(4,1)S(1)} %add_compare_fusion.2, ...), kind=kOutput, calls=%fused_computation.10.clone.1 | convolution fusion | flops 1097859072 | bytes 26280448 | tf_op jit(solution)/shard_map/cond/branch_1_fun/while/body/eval_jaxpr/hqk,khd->qhd/dot_general | solution.py:51
  472.8 47.3 %all-to-all-done.3 = bf16[4,256,1024]{2,1,0:T(8,128)(2,1)} async-done(((bf16[4,256,1024]{2,1,0:T(8,128)(2,1)}), bf16[4,256,1024]{2,1,0:T(8,128)(2,1)}, u32[]{:S(2)}, u32[]{:S(2)}) %all-to-all-start.3) | async-done | bytes 2097184 | tf_op jit(solution)/shard_map/all_to_all | solution.py:68
  (110 shorter events, 140.0 us)
Async XLA Ops:
  6.5 465.3 %copy-start = (f32[32,4096]{1,0:T(8,128)S(1)}, f32[32,4096]{1,0:T(8,128)}, u32[]{:S(2)}) copy-start(f32[32,4096]{1,0:T(8,128)} %param.13) | copy-start | bytes 1572868
  6.5 173.7 %all-gather.3.cloned.1.call-start = ((), (), s32[]{:S(2)}) async-start(), calls=%async_computation.4 | async-start | bytes 10485760 | tf_op jit(solution)/shard_map/all_gather | solution.py:29
  67.7 117.5 %all-gather.5.cloned.1.call-start = ((), (), s32[]{:S(2)}) async-start(), calls=%async_computation.5 | async-start | bytes 10485760 | tf_op jit(solution)/shard_map/all_gather | solution.py:30
  129.3 50.9 %all-to-all-start = ((bf16[256,4,1024]{0,2,1:T(8,128)(2,1)}), bf16[256,4,1024]{0,2,1:T(8,128)(2,1)S(1)}, u32[]{:S(2)}, u32[]{:S(2)}) async-start(bf16[256,4,1024]{0,2,1:T(8,128)(2,1)} %bitcast.78), calls=%async_computation | async-start | bytes 4194304 | tf_op jit(solution)/shard_map/all_to_all | solution.py:13
  205.6 12.1 %copy-start.1 = (f32[8,512,1024]{2,1,0:T(8,128)S(1)}, f32[8,512,1024]{2,1,0:T(8,128)}, u32[]{:S(2)}) copy-start(f32[8,512,1024]{2,1,0:T(8,128)} %get-tuple-element.305) | copy-start | bytes 50331652 | tf_op jit(solution)/shard_map/cond/branch_1_fun/while
  237.1 13.3 %copy-start.1 = (f32[8,512,1024]{2,1,0:T(8,128)S(1)}, f32[8,512,1024]{2,1,0:T(8,128)}, u32[]{:S(2)}) copy-start(f32[8,512,1024]{2,1,0:T(8,128)} %get-tuple-element.305) | copy-start | bytes 50331652 | tf_op jit(solution)/shard_map/cond/branch_1_fun/while
  270.5 13.3 %copy-start.1 = (f32[8,512,1024]{2,1,0:T(8,128)S(1)}, f32[8,512,1024]{2,1,0:T(8,128)}, u32[]{:S(2)}) copy-start(f32[8,512,1024]{2,1,0:T(8,128)} %get-tuple-element.305) | copy-start | bytes 50331652 | tf_op jit(solution)/shard_map/cond/branch_1_fun/while
  303.9 13.3 %copy-start.1 = (f32[8,512,1024]{2,1,0:T(8,128)S(1)}, f32[8,512,1024]{2,1,0:T(8,128)}, u32[]{:S(2)}) copy-start(f32[8,512,1024]{2,1,0:T(8,128)} %get-tuple-element.305) | copy-start | bytes 50331652 | tf_op jit(solution)/shard_map/cond/branch_1_fun/while
  337.3 13.3 %copy-start.1 = (f32[8,512,1024]{2,1,0:T(8,128)S(1)}, f32[8,512,1024]{2,1,0:T(8,128)}, u32[]{:S(2)}) copy-start(f32[8,512,1024]{2,1,0:T(8,128)} %get-tuple-element.305) | copy-start | bytes 50331652 | tf_op jit(solution)/shard_map/cond/branch_1_fun/while
  370.7 13.3 %copy-start.1 = (f32[8,512,1024]{2,1,0:T(8,128)S(1)}, f32[8,512,1024]{2,1,0:T(8,128)}, u32[]{:S(2)}) copy-start(f32[8,512,1024]{2,1,0:T(8,128)} %get-tuple-element.305) | copy-start | bytes 50331652 | tf_op jit(solution)/shard_map/cond/branch_1_fun/while
  404.1 13.3 %copy-start.1 = (f32[8,512,1024]{2,1,0:T(8,128)S(1)}, f32[8,512,1024]{2,1,0:T(8,128)}, u32[]{:S(2)}) copy-start(f32[8,512,1024]{2,1,0:T(8,128)} %get-tuple-element.305) | copy-start | bytes 50331652 | tf_op jit(solution)/shard_map/cond/branch_1_fun/while
  437.5 13.3 %copy-start.1 = (f32[8,512,1024]{2,1,0:T(8,128)S(1)}, f32[8,512,1024]{2,1,0:T(8,128)}, u32[]{:S(2)}) copy-start(f32[8,512,1024]{2,1,0:T(8,128)} %get-tuple-element.305) | copy-start | bytes 50331652 | tf_op jit(solution)/shard_map/cond/branch_1_fun/while
  462.4 8.9 %copy-start.2 = (s32[4]{0:T(128)S(1)}, s32[4]{0:T(128)}, u32[]{:S(2)}) copy-start(s32[4]{0:T(128)} %param.12) | copy-start | bytes 52
  466.7 53.4 %all-to-all-start.3 = ((bf16[4,256,1024]{2,1,0:T(8,128)(2,1)}), bf16[4,256,1024]{2,1,0:T(8,128)(2,1)}, u32[]{:S(2)}, u32[]{:S(2)}) async-start(bf16[4,256,1024]{2,1,0:T(8,128)(2,1)} %copy.42), calls=%async_computation.3 | async-start | bytes 4194304 | tf_op jit(solution)/shard_map/all_to_all | solution.py:68
Sparse Core Ops, SparseCore 0:
  67.8 57.4 all-gather.2
  126.9 58.2 all-gather.4
where the time goes:
time: 536 us; the launch traced here: 534 us
  matrix products  171 us (32%)
  blocking collectives  105 us (20%)
  waiting for transfers between devices  99.6 us (19%)
  local copies, waits for them, and re-layouts  84 us (16%)
  other arithmetic  51.5 us (10%)
  between operations  13.5 us (3%)
  starting transfers between devices  8.25 us (2%)
    dot_general x8, matrix products, one_block(): jnp.einsum('hqk,khd->qhd', expo.astype(jnp.bfloat16), value_block, prefer...  95.3 us
    dot_general x8, matrix products, one_block(): jnp.einsum('qhd,khd->hqk', query_three, key_block, preferred_element_type...  74.9 us
    all_to_all x1, blocking collectives, local(): lax.all_to_all(k_in[0], 'seq', split_axis=1, concat_axis=0, tiled=True)  54.5 us
    all_to_all x1, blocking collectives, local(): lax.all_to_all(v_in[0], 'seq', split_axis=1, concat_axis=0, tiled=True)  51 us
    all_to_all x1, waiting for transfers between devices, local(): lax.all_to_all(q_in[0], 'seq', split_axis=1, concat_axis=0, tiled=True)  47.3 us
    all_to_all x1, waiting for transfers between devices, local(): lax.all_to_all(attn, 'seq', split_axis=0, concat_axis=1, tiled=True)  47.3 us
    reduce_sum x8, other arithmetic, one_block(): total = total * shrink + jnp.sum(expo, axis=-1)  37 us
    dynamic_slice x16, local copies, waits for them, and re-layouts, one_block(): lax.dynamic_slice_in_dim(value_piece, offset, block, 0)  25.8 us
  transfers between devices with their start and end apart: 4, of which 3 were waited for; matrix products, arithmetic and copies ran while one was open for 2% of the time, Pallas kernels for 0%

commit v1 on v0

--- a/solution.py
+++ b/solution.py
@@ -8,11 +8,33 @@
 masked_score = -1e30
 
 
+def in_blocks(array, dim, size):
+    before, after = (array.shape[:dim], array.shape[dim + 1 :])
+    return jnp.moveaxis(array.reshape(*before, size, -1, *after), dim, 0)
+
+
+def laid_out(blocks, dim):
+    blocks = jnp.moveaxis(blocks, 0, dim)
+    shape = blocks.shape
+    return blocks.reshape(*shape[:dim], shape[dim] * shape[dim + 1], *shape[dim + 2 :])
+
+
+def pairwise_exchange(x, axis, split_dim, concat_dim):
+    size, place = (lax.axis_size(axis), lax.axis_index(axis))
+    tiles = in_blocks(x, split_dim, size)
+    finished = [tiles[place]]
+    for step in range(1, size):
+        sent = tiles[place ^ step]
+        finished.append(lax.ppermute(sent, axis, [(i, i ^ step) for i in range(size)]))
+    tiles = jnp.stack(finished)[place ^ jnp.arange(size)]
+    return laid_out(tiles, concat_dim)
+
+
 def local(q_in, k_in, v_in, timesteps, gate_table):
     head_rows, key_rows, value_rows = (
         lax.all_to_all(q_in[0], "seq", split_axis=1, concat_axis=0, tiled=True),
         lax.all_to_all(k_in[0], "seq", split_axis=1, concat_axis=0, tiled=True),
-        lax.all_to_all(v_in[0], "seq", split_axis=1, concat_axis=0, tiled=True),
+        pairwise_exchange(v_in[0], "seq", 1, 0),
     )
     length = head_rows.shape[0]
     columns = head_rows.shape[1]

time: 536 us -> 519 us (0.968)
  blocking collectives: 105 us -> 59.6 us
  waiting for transfers between devices: 99.6 us -> 134 us
  local copies, waits for them, and re-layouts: 84 us -> 70.4 us
  starting transfers between devices: 8.25 us -> 14.3 us
    all_to_all x1 -> x0, blocking collectives: 51 us -> none  [local(): lax.all_to_all(v_in[0], 'seq', split_axis=1, concat_axis=0, tiled=True)]
    ppermute x0 -> x3, waiting for transfers between devices: none -> 33.2 us  [pairwise_exchange(): lax.ppermute(sent, axis, [(i, i ^ step) for i in range(size)])]
    dynamic_slice x16 -> x8, local copies, waits for them, and re-layouts: 25.8 us -> 11.6 us  [one_block(): lax.dynamic_slice_in_dim(value_piece, offset, block, 0)]
    while x24 -> x72, local copies, waits for them, and re-layouts: 9.48 us -> 0.18 us
    all_gather x1, waiting for transfers between devices: 0.01 us -> 6 us  [local(): key_piece = lax.all_gather(key_rows, 'span', axis=0, tiled=True)]
    another operation x1 -> x6, local copies, waits for them, and re-layouts: 2.36 us -> 8.3 us
    ppermute x0 -> x3, starting transfers between devices: none -> 5.82 us  [pairwise_exchange(): lax.ppermute(sent, axis, [(i, i ^ step) for i in range(size)])]
    dynamic_slice x8 -> x16, local copies, waits for them, and re-layouts: 11.9 us -> 14.7 us  [one_block(): lax.dynamic_slice_in_dim(key_piece, offset, block, 0)]
  transfers between devices with their start and end apart: 4 -> 7, of which waited for: 3 -> 5; matrix products, arithmetic and copies ran while one was open for 2% -> 3% of each run, Pallas kernels for 0% -> 0%
where the time goes in v1:
time: 519 us; the launch traced here: 517 us
  matrix products  172 us (33%)
  waiting for transfers between devices  134 us (26%)
  local copies, waits for them, and re-layouts  70.4 us (14%)
  blocking collectives  59.6 us (11%)
  other arithmetic  53.3 us (10%)
  starting transfers between devices  14.3 us (3%)
  between operations  13.5 us (3%)
    dot_general x8, matrix products, one_block(): jnp.einsum('hqk,khd->qhd', expo.astype(jnp.bfloat16), value_block, prefer...  95.2 us
    dot_general x8, matrix products, one_block(): jnp.einsum('qhd,khd->hqk', query_three, key_block, preferred_element_type...  75.4 us
    all_to_all x1, blocking collectives, local(): lax.all_to_all(k_in[0], 'seq', split_axis=1, concat_axis=0, tiled=True)  59.6 us
    all_to_all x1, waiting for transfers between devices, local(): lax.all_to_all(q_in[0], 'seq', split_axis=1, concat_axis=0, tiled=True)  47.5 us
    all_to_all x1, waiting for transfers between devices, local(): lax.all_to_all(attn, 'seq', split_axis=0, concat_axis=1, tiled=True)  47.3 us
    reduce_sum x8, other arithmetic, one_block(): total = total * shrink + jnp.sum(expo, axis=-1)  37.1 us
    ppermute x3, waiting for transfers between devices, pairwise_exchange(): lax.ppermute(sent, axis, [(i, i ^ step) for i in range(size)])  33.2 us
    dynamic_slice x16, local copies, waits for them, and re-layouts, one_block(): lax.dynamic_slice_in_dim(key_piece, offset, block, 0)  14.7 us
  transfers between devices with their start and end apart: 7, of which 5 were waited for; matrix products, arithmetic and copies ran while one was open for 3% of the time, Pallas kernels for 0%

profile of v1, /device:TPU:0, one launch (start us, length us, event | category | flops | bytes accessed | tf_op | source)
XLA Modules:
  0.0 517.3 jit_solution(12024312783753112834)
XLA Ops:
  21.7 30.0 %collective-permute-done.1 = bf16[256,1024]{1,0:T(8,128)(2,1)S(1)} collective-permute-done((bf16[256,1024]{1,0:T(8,128)(2,1)S(1)}, bf16[256,1024]{1,0:T(8,128)(2,1)S(1)}, u32[]{:S(2)}, u32[]{:S(2)}) %collective-permute-start.1) | collective-permute-done | bytes 524320 | tf_op jit(solution)/shard_map/ppermute | solution.py:28
  65.3 59.6 %all_to_all.45 = bf16[256,4,1024]{0,2,1:T(8,128)(2,1)S(1)} all-to-all(bf16[256,4,1024]{0,2,1:T(8,128)(2,1)} %bitcast.90), channel_id=1, replica_groups=mesh['parts'=2,'span'=4,'seq'=4] {'seq'}, dimensions={1} | all-to-all | bytes 4194304 | tf_op jit(solution)/shard_map/all_to_all | solution.py:36
  135.3 47.5 %all-to-all-done = bf16[256,4,1024]{0,2,1:T(8,128)(2,1)S(1)} async-done(((bf16[256,4,1024]{0,2,1:T(8,128)(2,1)}), bf16[256,4,1024]{0,2,1:T(8,128)(2,1)S(1)}, u32[]{:S(2)}, u32[]{:S(2)}) %all-to-all-start) | async-done | bytes 2097184 | tf_op jit(solution)/shard_map/all_to_all | solution.py:35
  182.7 6.0 %all-gather.3.cloned.1.call-done = bf16[4096,1024]{1,0:T(8,128)(2,1)} async-done(((bf16[1024,1024]{1,0:T(8,128)(2,1)}), bf16[4096,1024]{1,0:T(8,128)(2,1)}) %all-gather.3.cloned.1.call-update) | async-done | bytes 8388624 | tf_op jit(solution)/shard_map/all_gather | solution.py:51
  188.7 251.7 %conditional.1 = (f32[8,1024]{1,0:T(8,128)}, f32[1024,8,128]{0,2,1:T(8,128)}) conditional(s32[]{:T(128)} %convert_element_type.44, () %tuple.27, (bf16[4,256,1024]{1,2,0:T(8,128)(2,1)S(1)}, s32[]{:T(128)}, bf16[4096,1024]{1,0:T(8,128)(2,1)}, bf16[4096,1024]{0,1:T(8,128)(2,1)}) %tuple.67), branch_computations={%region_0.0_spmd, %region_1.6_spmd} | conditional | flops 2205205504 | bytes 132647312 | solution.py:88
  195.0 245.4 %while.17 = (s32[]{:T(128)}, f32[8,1024]{1,0:T(8,128)S(1)}, f32[8,1024]{1,0:T(8,128)}, f32[1024,8,128]{0,2,1:T(8,128)}, s32[]{:T(128)}, /*index=5*/bf16[4096,102...) while((s32[]{:T(128)}, f32[8,1024]{1,0:T(8,128)S(1)}, ...), condition=%wide.region_5.5_spmd.clone, body=%wide.region_2.4_spmd.clone.sunk | while | flops 2205205504 | bytes 120064280 | solution.py:83
  196.8 9.4 %bitcast_reduce_fusion.2 = (f32[8,1024]{1,0:T(8,128)S(1)}, f32[8,512,1024]{2,1,0:T(8,128)}) fusion(pred[512]{0:T(512)(128)(4,1)S(1)} %add_compare_fusion.2, bf16[512,8,128]{0,2,1:T(8,128)(2,1)S(1)} %bitcast.81, bf16[1024,8,128]{2,0,1:T(8,128)(2,1)} %get-tuple-element.348), kind=kOutput, calls=%fused_computation.2.clone.1 | convolution fusion | flops 1086316544 | bytes 19956224 | tf_op jit(solution)/shard_map/cond/branch_1_fun/while/body/eval_jaxpr/qhd,khd->hqk/dot_general | solution.py:64
  207.8 10.9 %bitcast_add_fusion.2 = f32[1024,8,128]{0,2,1:T(8,128)} fusion(f32[1024,8,128]{0,2,1:T(8,128)} %get-tuple-element.333, bf16[512,8,128]{0,2,1:T(8,128)(2,1)S(1)} %bitcast.82, f32[8,512,1024]{2,1,0:T(8,128)} %get-tuple-element.316, f32[8,1024]{1,0:T(8,128)S(1)} %get-tuple-element.343, pred[512]{0:T(512)(128)(4,1)S(1)} %add_compare_fusion.2, ...), kind=kOutput, calls=%fused_computation.11.clone.1 | convolution fusion | flops 1097859072 | bytes 26280448 | tf_op jit(solution)/shard_map/cond/branch_1_fun/while/body/eval_jaxpr/hqk,khd->qhd/dot_general | solution.py:73
  225.8 9.4 %bitcast_reduce_fusion.2 = (f32[8,1024]{1,0:T(8,128)S(1)}, f32[8,512,1024]{2,1,0:T(8,128)}) fusion(pred[512]{0:T(512)(128)(4,1)S(1)} %add_compare_fusion.2, bf16[512,8,128]{0,2,1:T(8,128)(2,1)S(1)} %bitcast.81, bf16[1024,8,128]{2,0,1:T(8,128)(2,1)} %get-tuple-element.348), kind=kOutput, calls=%fused_computation.2.clone.1 | convolution fusion | flops 1086316544 | bytes 19956224 | tf_op jit(solution)/shard_map/cond/branch_1_fun/while/body/eval_jaxpr/qhd,khd->hqk/dot_general | solution.py:64
  236.8 12.0 %bitcast_add_fusion.2 = f32[1024,8,128]{0,2,1:T(8,128)} fusion(f32[1024,8,128]{0,2,1:T(8,128)} %get-tuple-element.333, bf16[512,8,128]{0,2,1:T(8,128)(2,1)S(1)} %bitcast.82, f32[8,512,1024]{2,1,0:T(8,128)} %get-tuple-element.316, f32[8,1024]{1,0:T(8,128)S(1)} %get-tuple-element.343, pred[512]{0:T(512)(128)(4,1)S(1)} %add_compare_fusion.2, ...), kind=kOutput, calls=%fused_computation.11.clone.1 | convolution fusion | flops 1097859072 | bytes 26280448 | tf_op jit(solution)/shard_map/cond/branch_1_fun/while/body/eval_jaxpr/hqk,khd->qhd/dot_general | solution.py:73
  256.7 9.4 %bitcast_reduce_fusion.2 = (f32[8,1024]{1,0:T(8,128)S(1)}, f32[8,512,1024]{2,1,0:T(8,128)}) fusion(pred[512]{0:T(512)(128)(4,1)S(1)} %add_compare_fusion.2, bf16[512,8,128]{0,2,1:T(8,128)(2,1)S(1)} %bitcast.81, bf16[1024,8,128]{2,0,1:T(8,128)(2,1)} %get-tuple-element.348), kind=kOutput, calls=%fused_computation.2.clone.1 | convolution fusion | flops 1086316544 | bytes 19956224 | tf_op jit(solution)/shard_map/cond/branch_1_fun/while/body/eval_jaxpr/qhd,khd->hqk/dot_general | solution.py:64
  267.7 12.0 %bitcast_add_fusion.2 = f32[1024,8,128]{0,2,1:T(8,128)} fusion(f32[1024,8,128]{0,2,1:T(8,128)} %get-tuple-element.333, bf16[512,8,128]{0,2,1:T(8,128)(2,1)S(1)} %bitcast.82, f32[8,512,1024]{2,1,0:T(8,128)} %get-tuple-element.316, f32[8,1024]{1,0:T(8,128)S(1)} %get-tuple-element.343, pred[512]{0:T(512)(128)(4,1)S(1)} %add_compare_fusion.2, ...), kind=kOutput, calls=%fused_computation.11.clone.1 | convolution fusion | flops 1097859072 | bytes 26280448 | tf_op jit(solution)/shard_map/cond/branch_1_fun/while/body/eval_jaxpr/hqk,khd->qhd/dot_general | solution.py:73
  287.7 9.4 %bitcast_reduce_fusion.2 = (f32[8,1024]{1,0:T(8,128)S(1)}, f32[8,512,1024]{2,1,0:T(8,128)}) fusion(pred[512]{0:T(512)(128)(4,1)S(1)} %add_compare_fusion.2, bf16[512,8,128]{0,2,1:T(8,128)(2,1)S(1)} %bitcast.81, bf16[1024,8,128]{2,0,1:T(8,128)(2,1)} %get-tuple-element.348), kind=kOutput, calls=%fused_computation.2.clone.1 | convolution fusion | flops 1086316544 | bytes 19956224 | tf_op jit(solution)/shard_map/cond/branch_1_fun/while/body/eval_jaxpr/qhd,khd->hqk/dot_general | solution.py:64
  298.6 12.0 %bitcast_add_fusion.2 = f32[1024,8,128]{0,2,1:T(8,128)} fusion(f32[1024,8,128]{0,2,1:T(8,128)} %get-tuple-element.333, bf16[512,8,128]{0,2,1:T(8,128)(2,1)S(1)} %bitcast.82, f32[8,512,1024]{2,1,0:T(8,128)} %get-tuple-element.316, f32[8,1024]{1,0:T(8,128)S(1)} %get-tuple-element.343, pred[512]{0:T(512)(128)(4,1)S(1)} %add_compare_fusion.2, ...), kind=kOutput, calls=%fused_computation.11.clone.1 | convolution fusion | flops 1097859072 | bytes 26280448 | tf_op jit(solution)/shard_map/cond/branch_1_fun/while/body/eval_jaxpr/hqk,khd->qhd/dot_general | solution.py:73
  318.6 9.4 %bitcast_reduce_fusion.2 = (f32[8,1024]{1,0:T(8,128)S(1)}, f32[8,512,1024]{2,1,0:T(8,128)}) fusion(pred[512]{0:T(512)(128)(4,1)S(1)} %add_compare_fusion.2, bf16[512,8,128]{0,2,1:T(8,128)(2,1)S(1)} %bitcast.81, bf16[1024,8,128]{2,0,1:T(8,128)(2,1)} %get-tuple-element.348), kind=kOutput, calls=%fused_computation.2.clone.1 | convolution fusion | flops 1086316544 | bytes 19956224 | tf_op jit(solution)/shard_map/cond/branch_1_fun/while/body/eval_jaxpr/qhd,khd->hqk/dot_general | solution.py:64
  329.5 12.0 %bitcast_add_fusion.2 = f32[1024,8,128]{0,2,1:T(8,128)} fusion(f32[1024,8,128]{0,2,1:T(8,128)} %get-tuple-element.333, bf16[512,8,128]{0,2,1:T(8,128)(2,1)S(1)} %bitcast.82, f32[8,512,1024]{2,1,0:T(8,128)} %get-tuple-element.316, f32[8,1024]{1,0:T(8,128)S(1)} %get-tuple-element.343, pred[512]{0:T(512)(128)(4,1)S(1)} %add_compare_fusion.2, ...), kind=kOutput, calls=%fused_computation.11.clone.1 | convolution fusion | flops 1097859072 | bytes 26280448 | tf_op jit(solution)/shard_map/cond/branch_1_fun/while/body/eval_jaxpr/hqk,khd->qhd/dot_general | solution.py:73
  341.6 4.6 fusion.38
  349.5 9.4 %bitcast_reduce_fusion.2 = (f32[8,1024]{1,0:T(8,128)S(1)}, f32[8,512,1024]{2,1,0:T(8,128)}) fusion(pred[512]{0:T(512)(128)(4,1)S(1)} %add_compare_fusion.2, bf16[512,8,128]{0,2,1:T(8,128)(2,1)S(1)} %bitcast.81, bf16[1024,8,128]{2,0,1:T(8,128)(2,1)} %get-tuple-element.348), kind=kOutput, calls=%fused_computation.2.clone.1 | convolution fusion | flops 1086316544 | bytes 19956224 | tf_op jit(solution)/shard_map/cond/branch_1_fun/while/body/eval_jaxpr/qhd,khd->hqk/dot_general | solution.py:64
  360.4 12.0 %bitcast_add_fusion.2 = f32[1024,8,128]{0,2,1:T(8,128)} fusion(f32[1024,8,128]{0,2,1:T(8,128)} %get-tuple-element.333, bf16[512,8,128]{0,2,1:T(8,128)(2,1)S(1)} %bitcast.82, f32[8,512,1024]{2,1,0:T(8,128)} %get-tuple-element.316, f32[8,1024]{1,0:T(8,128)S(1)} %get-tuple-element.343, pred[512]{0:T(512)(128)(4,1)S(1)} %add_compare_fusion.2, ...), kind=kOutput, calls=%fused_computation.11.clone.1 | convolution fusion | flops 1097859072 | bytes 26280448 | tf_op jit(solution)/shard_map/cond/branch_1_fun/while/body/eval_jaxpr/hqk,khd->qhd/dot_general | solution.py:73
  380.4 9.4 %bitcast_reduce_fusion.2 = (f32[8,1024]{1,0:T(8,128)S(1)}, f32[8,512,1024]{2,1,0:T(8,128)}) fusion(pred[512]{0:T(512)(128)(4,1)S(1)} %add_compare_fusion.2, bf16[512,8,128]{0,2,1:T(8,128)(2,1)S(1)} %bitcast.81, bf16[1024,8,128]{2,0,1:T(8,128)(2,1)} %get-tuple-element.348), kind=kOutput, calls=%fused_computation.2.clone.1 | convolution fusion | flops 1086316544 | bytes 19956224 | tf_op jit(solution)/shard_map/cond/branch_1_fun/while/body/eval_jaxpr/qhd,khd->hqk/dot_general | solution.py:64
  391.4 12.0 %bitcast_add_fusion.2 = f32[1024,8,128]{0,2,1:T(8,128)} fusion(f32[1024,8,128]{0,2,1:T(8,128)} %get-tuple-element.333, bf16[512,8,128]{0,2,1:T(8,128)(2,1)S(1)} %bitcast.82, f32[8,512,1024]{2,1,0:T(8,128)} %get-tuple-element.316, f32[8,1024]{1,0:T(8,128)S(1)} %get-tuple-element.343, pred[512]{0:T(512)(128)(4,1)S(1)} %add_compare_fusion.2, ...), kind=kOutput, calls=%fused_computation.11.clone.1 | convolution fusion | flops 1097859072 | bytes 26280448 | tf_op jit(solution)/shard_map/cond/branch_1_fun/while/body/eval_jaxpr/hqk,khd->qhd/dot_general | solution.py:73
  411.3 9.4 %bitcast_reduce_fusion.2 = (f32[8,1024]{1,0:T(8,128)S(1)}, f32[8,512,1024]{2,1,0:T(8,128)}) fusion(pred[512]{0:T(512)(128)(4,1)S(1)} %add_compare_fusion.2, bf16[512,8,128]{0,2,1:T(8,128)(2,1)S(1)} %bitcast.81, bf16[1024,8,128]{2,0,1:T(8,128)(2,1)} %get-tuple-element.348), kind=kOutput, calls=%fused_computation.2.clone.1 | convolution fusion | flops 1086316544 | bytes 19956224 | tf_op jit(solution)/shard_map/cond/branch_1_fun/while/body/eval_jaxpr/qhd,khd->hqk/dot_general | solution.py:64
  422.3 12.0 %bitcast_add_fusion.2 = f32[1024,8,128]{0,2,1:T(8,128)} fusion(f32[1024,8,128]{0,2,1:T(8,128)} %get-tuple-element.333, bf16[512,8,128]{0,2,1:T(8,128)(2,1)S(1)} %bitcast.82, f32[8,512,1024]{2,1,0:T(8,128)} %get-tuple-element.316, f32[8,1024]{1,0:T(8,128)S(1)} %get-tuple-element.343, pred[512]{0:T(512)(128)(4,1)S(1)} %add_compare_fusion.2, ...), kind=kOutput, calls=%fused_computation.11.clone.1 | convolution fusion | flops 1097859072 | bytes 26280448 | tf_op jit(solution)/shard_map/cond/branch_1_fun/while/body/eval_jaxpr/hqk,khd->qhd/dot_general | solution.py:73
  456.4 47.3 %all-to-all-done.2 = bf16[4,256,1024]{2,1,0:T(8,128)(2,1)} async-done(((bf16[4,256,1024]{2,1,0:T(8,128)(2,1)}), bf16[4,256,1024]{2,1,0:T(8,128)(2,1)}, u32[]{:S(2)}, u32[]{:S(2)}) %all-to-all-start.2) | async-done | bytes 2097184 | tf_op jit(solution)/shard_map/all_to_all | solution.py:90
  (184 shorter events, 137.5 us)
Async XLA Ops:
  6.5 448.9 %copy-start = (f32[32,4096]{1,0:T(8,128)S(1)}, f32[32,4096]{1,0:T(8,128)}, u32[]{:S(2)}) copy-start(f32[32,4096]{1,0:T(8,128)} %param.13) | copy-start | bytes 1572868
  6.5 176.2 %all-gather.5.cloned.1.call-start = ((), (), s32[]{:S(2)}) async-start(), calls=%async_computation.4 | async-start | bytes 10485760 | tf_op jit(solution)/shard_map/all_gather | solution.py:52
  12.3 39.4 %collective-permute-start.1 = (bf16[256,1024]{1,0:T(8,128)(2,1)S(1)}, bf16[256,1024]{1,0:T(8,128)(2,1)S(1)}, u32[]{:S(2)}, u32[]{:S(2)}) collective-permute-start(bf16[256,1024]{1,0:T(8,128)(2,1)S(1)} %bitcast.93), channel_id=1, source_target_pairs={{0,2},{1,3},{2,0},{3,1},{4,6},{5,7},{6,4},{7,5},{8,10},{9,11},{10,... | collective-permute-start | bytes 1572872 | tf_op jit(solution)/shard_map/ppermute | solution.py:28
  17.7 34.0 %collective-permute-start.2 = (bf16[256,1024]{1,0:T(8,128)(2,1)S(1)}, bf16[256,1024]{1,0:T(8,128)(2,1)}, u32[]{:S(2)}, u32[]{:S(2)}) collective-permute-start(bf16[256,1024]{1,0:T(8,128)(2,1)S(1)} %bitcast.94), channel_id=1, source_target_pairs={{0,3},{1,2},{2,1},{3,0},{4,7},{5,6},{6,5},{7,4},{8,11},{9,10},{10,... | collective-permute-start | bytes 1572872 | tf_op jit(solution)/shard_map/ppermute | solution.py:28
  20.3 34.6 %collective-permute-start = (bf16[256,1024]{1,0:T(8,128)(2,1)S(1)}, bf16[256,1024]{1,0:T(8,128)(2,1)}, u32[]{:S(2)}, u32[]{:S(2)}) collective-permute-start(bf16[256,1024]{1,0:T(8,128)(2,1)S(1)} %bitcast.95), channel_id=1, source_target_pairs={{0,1},{1,0},{2,3},{3,2},{4,5},{5,4},{6,7},{7,6},{8,9},{9,8},{10,11... | collective-permute-start | bytes 1572872 | tf_op jit(solution)/shard_map/ppermute | solution.py:28
  62.8 125.9 %all-gather.3.cloned.1.call-start = ((), (), s32[]{:S(2)}) async-start(), calls=%async_computation.3 | async-start | bytes 10485760 | tf_op jit(solution)/shard_map/all_gather | solution.py:51
  131.5 51.3 %all-to-all-start = ((bf16[256,4,1024]{0,2,1:T(8,128)(2,1)}), bf16[256,4,1024]{0,2,1:T(8,128)(2,1)S(1)}, u32[]{:S(2)}, u32[]{:S(2)}) async-start(bf16[256,4,1024]{0,2,1:T(8,128)(2,1)} %bitcast.86), calls=%async_computation | async-start | bytes 4194304 | tf_op jit(solution)/shard_map/all_to_all | solution.py:35
  206.3 12.4 %slice-start = ((s8[16777216]{0:T(1024)(128)(4,1)}), s8[4194304]{0:T(1024)(128)(4,1)S(1)}, s32[]{:S(2)}) async-start(s8[16777216]{0:T(1024)(128)(4,1)} %bitcast.79), calls=%async_computation.5 | async-start | bytes 8388608 | tf_op jit(solution)/shard_map/cond/branch_1_fun/while
  235.3 13.5 %slice-start = ((s8[16777216]{0:T(1024)(128)(4,1)}), s8[4194304]{0:T(1024)(128)(4,1)S(1)}, s32[]{:S(2)}) async-start(s8[16777216]{0:T(1024)(128)(4,1)} %bitcast.79), calls=%async_computation.5 | async-start | bytes 8388608 | tf_op jit(solution)/shard_map/cond/branch_1_fun/while
  236.7 12.1 %slice-start.1 = ((s8[16777216]{0:T(1024)(128)(4,1)}), s8[4194304]{0:T(1024)(128)(4,1)S(1)}, s32[]{:S(2)}) async-start(s8[16777216]{0:T(1024)(128)(4,1)} %bitcast.79), calls=%async_computation.6 | async-start | bytes 8388608 | tf_op jit(solution)/shard_map/cond/branch_1_fun/while
  266.2 13.5 %slice-start = ((s8[16777216]{0:T(1024)(128)(4,1)}), s8[4194304]{0:T(1024)(128)(4,1)S(1)}, s32[]{:S(2)}) async-start(s8[16777216]{0:T(1024)(128)(4,1)} %bitcast.79), calls=%async_computation.5 | async-start | bytes 8388608 | tf_op jit(solution)/shard_map/cond/branch_1_fun/while
  267.6 12.1 %slice-start.1 = ((s8[16777216]{0:T(1024)(128)(4,1)}), s8[4194304]{0:T(1024)(128)(4,1)S(1)}, s32[]{:S(2)}) async-start(s8[16777216]{0:T(1024)(128)(4,1)} %bitcast.79), calls=%async_computation.6 | async-start | bytes 8388608 | tf_op jit(solution)/shard_map/cond/branch_1_fun/while
  267.7 12.1 %slice-start.2 = ((s8[16777216]{0:T(1024)(128)(4,1)}), s8[4194304]{0:T(1024)(128)(4,1)S(1)}, s32[]{:S(2)}) async-start(s8[16777216]{0:T(1024)(128)(4,1)} %bitcast.79), calls=%async_computation.7 | async-start | bytes 8388608 | tf_op jit(solution)/shard_map/cond/branch_1_fun/while
  297.1 13.5 %slice-start = ((s8[16777216]{0:T(1024)(128)(4,1)}), s8[4194304]{0:T(1024)(128)(4,1)S(1)}, s32[]{:S(2)}) async-start(s8[16777216]{0:T(1024)(128)(4,1)} %bitcast.79), calls=%async_computation.5 | async-start | bytes 8388608 | tf_op jit(solution)/shard_map/cond/branch_1_fun/while
  298.6 12.1 %slice-start.1 = ((s8[16777216]{0:T(1024)(128)(4,1)}), s8[4194304]{0:T(1024)(128)(4,1)S(1)}, s32[]{:S(2)}) async-start(s8[16777216]{0:T(1024)(128)(4,1)} %bitcast.79), calls=%async_computation.6 | async-start | bytes 8388608 | tf_op jit(solution)/shard_map/cond/branch_1_fun/while
  328.0 13.5 %slice-start = ((s8[16777216]{0:T(1024)(128)(4,1)}), s8[4194304]{0:T(1024)(128)(4,1)S(1)}, s32[]{:S(2)}) async-start(s8[16777216]{0:T(1024)(128)(4,1)} %bitcast.79), calls=%async_computation.5 | async-start | bytes 8388608 | tf_op jit(solution)/shard_map/cond/branch_1_fun/while
  329.5 12.1 %slice-start.1 = ((s8[16777216]{0:T(1024)(128)(4,1)}), s8[4194304]{0:T(1024)(128)(4,1)S(1)}, s32[]{:S(2)}) async-start(s8[16777216]{0:T(1024)(128)(4,1)} %bitcast.79), calls=%async_computation.6 | async-start | bytes 8388608 | tf_op jit(solution)/shard_map/cond/branch_1_fun/while
  358.9 13.5 %slice-start = ((s8[16777216]{0:T(1024)(128)(4,1)}), s8[4194304]{0:T(1024)(128)(4,1)S(1)}, s32[]{:S(2)}) async-start(s8[16777216]{0:T(1024)(128)(4,1)} %bitcast.79), calls=%async_computation.5 | async-start | bytes 8388608 | tf_op jit(solution)/shard_map/cond/branch_1_fun/while
  360.4 12.1 %slice-start.1 = ((s8[16777216]{0:T(1024)(128)(4,1)}), s8[4194304]{0:T(1024)(128)(4,1)S(1)}, s32[]{:S(2)}) async-start(s8[16777216]{0:T(1024)(128)(4,1)} %bitcast.79), calls=%async_computation.6 | async-start | bytes 8388608 | tf_op jit(solution)/shard_map/cond/branch_1_fun/while
  389.9 13.5 %slice-start = ((s8[16777216]{0:T(1024)(128)(4,1)}), s8[4194304]{0:T(1024)(128)(4,1)S(1)}, s32[]{:S(2)}) async-start(s8[16777216]{0:T(1024)(128)(4,1)} %bitcast.79), calls=%async_computation.5 | async-start | bytes 8388608 | tf_op jit(solution)/shard_map/cond/branch_1_fun/while
  391.3 12.1 %slice-start.1 = ((s8[16777216]{0:T(1024)(128)(4,1)}), s8[4194304]{0:T(1024)(128)(4,1)S(1)}, s32[]{:S(2)}) async-start(s8[16777216]{0:T(1024)(128)(4,1)} %bitcast.79), calls=%async_computation.6 | async-start | bytes 8388608 | tf_op jit(solution)/shard_map/cond/branch_1_fun/while
  420.8 13.5 %slice-start = ((s8[16777216]{0:T(1024)(128)(4,1)}), s8[4194304]{0:T(1024)(128)(4,1)S(1)}, s32[]{:S(2)}) async-start(s8[16777216]{0:T(1024)(128)(4,1)} %bitcast.79), calls=%async_computation.5 | async-start | bytes 8388608 | tf_op jit(solution)/shard_map/cond/branch_1_fun/while
  422.3 12.1 %slice-start.1 = ((s8[16777216]{0:T(1024)(128)(4,1)}), s8[4194304]{0:T(1024)(128)(4,1)S(1)}, s32[]{:S(2)}) async-start(s8[16777216]{0:T(1024)(128)(4,1)} %bitcast.79), calls=%async_computation.6 | async-start | bytes 8388608 | tf_op jit(solution)/shard_map/cond/branch_1_fun/while
  450.3 53.4 %all-to-all-start.2 = ((bf16[4,256,1024]{2,1,0:T(8,128)(2,1)}), bf16[4,256,1024]{2,1,0:T(8,128)(2,1)}, u32[]{:S(2)}, u32[]{:S(2)}) async-start(bf16[4,256,1024]{2,1,0:T(8,128)(2,1)} %copy.62), calls=%async_computation.2 | async-start | bytes 4194304 | tf_op jit(solution)/shard_map/all_to_all | solution.py:90
  (19 other events, 205.9 us)
Sparse Core Ops, SparseCore 0:
  62.9 65.8 all-gather.4
  130.4 58.2 all-gather.2
